TPU v7x, 32 devices: a whole 2x2x4 slice. The times are simulated.
32 devices in a mesh: groups: 2 (over y), tile: 4 (over z), segment: 2 (over core), mp: 2 (over x).
Axes of the slice: x: 2, y: 2, z: 4, core: 2. Of those that a mesh axis runs over, the one named last changes fastest.
Arguments:
- spectra: bfloat16 [2, 64, 48, 224], P(None, ('groups', 'tile')), parts along dimension 1, may hold values from -6 to 6
- valid: int32 [2, 64], P(None, 'groups'), parts along dimension 1, may hold values from 1 to 48, as said below
- project: bfloat16 [224, 16], replicated, may hold values from -0.375 to 0.375
- enc_in: bfloat16 [768, 3072], P(None, 'mp'), may hold values from -0.21875 to 0.21875
- enc_out: bfloat16 [3072, 768], P('mp'), may hold values from -0.109375 to 0.109375
- tok_embed: bfloat16 [48, 2048], replicated, may hold values from -0.875 to 0.875
- band_embed: bfloat16 [16, 2048], P('tile'), may hold values from -3 to 3
- dec_in: bfloat16 [2048, 8192], P('tile', 'mp'), may hold values from -0.125 to 0.125
- dec_out: bfloat16 [8192, 2048], P('mp', 'tile'), may hold values from -0.0625 to 0.0625
- head: bfloat16 [2048, 672], P('tile', 'mp'), may hold values from -0.125 to 0.125
Outputs:
- grad_project: float32 [448, 16], P(('groups', 'tile', 'segment')), parts along dimension 0
- grad_enc_in: float32 [1536, 3072], P(('groups', 'tile', 'segment'), 'mp'), parts along dimension 0
- grad_enc_out: float32 [6144, 768], P(('groups', 'mp'), ('tile', 'segment')), parts along dimension 0
There are 2 independent parts, one for each index of `groups`. A program takes and returns all parts, laid end to end along the dimension named above; an argument that names none is the same for every part. Nothing has to cross between parts.
Inputs may be any that keep to these rules, and one draw needn't show every extreme that they name: Pixels of patch n in micro-batch m with index below valid[m, n] count in the loss.
All inputs are finite; a program needn't handle non-finite values.
Results may differ from a plain program's by a relative error of at most 0.018.
Values may be sent and summed in bfloat16 or wider, within the bound.
A program may use at most 128 MiB of HBM per device.

v0:
```python
import jax
import jax.numpy as jnp
from jax import lax
from jax.sharding import PartitionSpec as P

BF = jnp.bfloat16
F32 = jnp.float32


def inv_rms(values):
    return lax.rsqrt(jnp.mean(values * values, axis=-1, keepdims=True) + 1e-05)


def rms_back(values, gradient):
    scaling = inv_rms(values)
    normed = values * scaling
    return scaling * (gradient - normed * jnp.mean(gradient * normed, axis=-1, keepdims=True))


def gelu(v):
    return 0.5 * v * (1 + jnp.tanh(0.7978845608028654 * (v + 0.044715 * v * v * v)))


def gelu_and_slope(v):
    square = v * v
    t = jnp.tanh(0.7978845608028654 * v * (1 + 0.044715 * square))
    half = 0.5 * (1 + t)
    slope = half + 0.5 * v * (1 - t * t) * 0.7978845608028654 * (1 + 3 * 0.044715 * square)
    return (v * half, slope)


def dot(a, b):
    return jnp.dot(a, b, preferred_element_type=F32)


def dot_t(a, b):
    return lax.dot_general(a, b, (((1,), (1,)), ((), ())), preferred_element_type=F32)


def t_dot(a, b):
    return lax.dot_general(a, b, (((0,), (0,)), ((), ())), preferred_element_type=F32)


def body(spectra, valid, project, enc_in, enc_out, tok_embed, band_embed, dec_in, dec_out, head):
    tile, seg, mp = (lax.axis_index(a) for a in ("tile", "segment", "mp"))
    T, S, M = (lax.axis_size(a) for a in ("tile", "segment", "mp"))
    batches, per_tile, pixels, bands = spectra.shape
    codes = project.shape[1]
    width = bands // codes
    local = batches * per_tile
    share = local // (S * M)
    rows = T * local
    student = codes * pixels
    dim = tok_embed.shape[1]
    dt = dec_in.shape[0]
    hid = dec_in.shape[1] // S
    once = jnp.logical_and(seg == 0, mp == 0).astype(F32)
    patches = spectra.reshape(local, pixels, bands)
    flat = patches.reshape(local * pixels, bands)
    feat_local = (
        dot(flat, project)
        .astype(BF)
        .reshape(local, pixels, codes)
        .transpose(0, 2, 1)
        .reshape(local, student)
    )
    feats = lax.all_gather(feat_local, "tile")
    feats = feats.reshape(T, S, M, share, student).transpose(1, 2, 0, 3, 4).reshape(rows, student)
    band_all = lax.all_gather(band_embed, "tile", tiled=True)
    head_full = lax.all_gather(head, "mp", axis=1, tiled=True)
    embed = jnp.concatenate([tok_embed, band_all], axis=0)
    embed_z = lax.dynamic_slice_in_dim(embed, tile * dt, dt, 1)
    d_in = lax.dynamic_slice_in_dim(dec_in, seg * hid, hid, 1)
    d_out = lax.dynamic_slice_in_dim(dec_out, seg * hid, hid, 0)
    folded = lax.psum(dot(embed_z, d_in).astype(BF), "tile")
    fold_tok, fold_band = (folded[:pixels], folded[pixels:])
    feats32 = feats.astype(F32)
    normed = (feats32 * inv_rms(feats32)).astype(BF)
    pre_act, pre_slope = gelu_and_slope(dot(normed, enc_in))
    act_out = pre_act.astype(BF)
    summed = lax.psum(dot(act_out, enc_out).astype(BF), "mp").astype(F32)
    encoded = (feats32 + summed).astype(BF)
    tokens = rows * codes
    tok = encoded.reshape(tokens, pixels)
    embedded = (
        (dot(tok, tok_embed).reshape(rows, codes, dim) + band_all.astype(F32))
        .reshape(tokens, dim)
        .astype(BF)
    )
    scaling = inv_rms(embedded.astype(F32))
    hid_pre = scaling * (
        dot(tok, fold_tok).reshape(rows, codes, hid) + fold_band.astype(F32)
    ).reshape(tokens, hid)
    hid_act, hid_slope = gelu_and_slope(hid_pre)
    embedded_z = lax.dynamic_slice_in_dim(embedded, tile * dt, dt, 1)
    decoded = (once * embedded_z.astype(F32) + dot(hid_act.astype(BF), d_out)).astype(BF)
    partial = dot(decoded, head_full).astype(BF)
    own = lax.psum_scatter(
        partial.reshape(S * M, T, share * codes, -1), ("segment", "mp"), scatter_dimension=0
    )
    own = lax.psum_scatter(own, "tile", scatter_dimension=0).astype(F32)
    quarter = (seg * M + mp) * share
    own_patches = lax.dynamic_slice_in_dim(patches, quarter, share, 0)
    target = (
        own_patches.reshape(share, pixels, codes, width)
        .transpose(0, 2, 1, 3)
        .reshape(share * codes, -1)
    )
    total_valid = jnp.sum(valid.astype(F32))
    loss_scale = 2.0 * batches * valid.shape[1] / total_valid
    own_valid = lax.dynamic_slice_in_dim(valid, tile * per_tile, per_tile, 1).reshape(local)
    own_valid = lax.dynamic_slice_in_dim(own_valid, quarter, share, 0)
    column = jnp.arange(pixels * width, dtype=jnp.int32) // width
    mask = (column[None, :] < jnp.repeat(own_valid, codes)[:, None]).astype(F32)
    grad_own = (loss_scale * mask * (own - target.astype(F32))).astype(BF)
    grad_rebuilt = lax.all_gather(lax.all_gather(grad_own, "tile"), ("segment", "mp")).reshape(
        tokens, -1
    )
    grad_decoded = dot_t(grad_rebuilt, head_full).astype(BF)
    grad_hid = hid_slope * dot_t(grad_decoded, d_out)
    tok_z = lax.dynamic_slice_in_dim(tok_embed, tile * dt, dt, 1)
    unit_tok = dot_t((embedded.astype(F32) * scaling).astype(BF), tok_embed)
    along = jnp.sum(grad_hid * hid_pre, axis=1, keepdims=True) / dim
    grad_tok = scaling * (dot_t(grad_hid.astype(BF), fold_tok) - unit_tok * along)
    grad_tok = grad_tok + once * dot_t(grad_decoded, tok_z)
    grad_encoded = lax.psum(grad_tok.reshape(rows, student).astype(BF), ("tile", "segment", "mp"))
    grad_act = (pre_slope * dot_t(grad_encoded, enc_out)).astype(BF)
    columns = student // (T * S)
    start = (tile * S + seg) * columns
    grad_out = t_dot(act_out, lax.dynamic_slice_in_dim(grad_encoded, start, columns, 1))
    grad_in = t_dot(lax.dynamic_slice_in_dim(normed, start, columns, 1), grad_act)
    grad_normed = lax.psum(dot_t(grad_act, enc_in).astype(BF), "mp").astype(F32)
    own_rows = lambda a: lax.dynamic_slice_in_dim(
        a.reshape(S * M, T, share, student), tile, 1, 1
    ).reshape(local, student)
    grad_feat = (
        own_rows(grad_encoded).astype(F32) + rms_back(feat_local.astype(F32), own_rows(grad_normed))
    ).astype(BF)
    grad_codes = grad_feat.reshape(local, codes, pixels).transpose(0, 2, 1).reshape(-1, codes)
    grad_proj = jnp.sum(lax.all_gather(t_dot(flat, grad_codes), "tile"), axis=0)
    proj_rows = bands // (T * S)
    grad_proj = lax.dynamic_slice_in_dim(grad_proj, (tile * S + seg) * proj_rows, proj_rows, 0)
    return (grad_proj, grad_in, grad_out)


def solution(mesh):
    placed = (
        P(None, ("groups", "tile"), None, None),
        P(None, "groups"),
        P(),
        P(None, "mp"),
        P("mp", None),
        P(),
        P("tile", None),
        P("tile", "mp"),
        P("mp", "tile"),
        P("tile", "mp"),
    )
    return jax.shard_map(
        body,
        mesh=mesh,
        in_specs=placed,
        out_specs=(
            P(("groups", "tile", "segment"), None),
            P(("groups", "tile", "segment"), "mp"),
            P(("groups", "mp"), ("tile", "segment")),
        ),
        check_vma=False,
    )
```

profile of v0, /device:TPU:0, one launch (start us, length us, event | category | flops | bytes accessed | tf_op | source)
XLA Modules:
  0.0 350.5 jit_solution(10092934858017082224)
XLA Ops:
  9.6 15.0 %all_gather.25 = bf16[4,16,768]{2,1,0:T(8,128)(2,1)S(1)} all-gather(bf16[1,16,768]{2,1,0:T(8,128)(2,1)S(1)} %all_gather_reshape.3), channel_id=1, replica_groups=mesh['groups'=2,'tile'=4,'segment'=2,'mp'=2] {'tile'}, dimensions={0}, use_global_device_ids=true | all-gather | bytes 122880 | tf_op jit(solution)/shard_map/all_gather | solution.py:67
  25.2 2.2 fusion.50
  29.5 13.3 %all-gather.2 = bf16[4,4,2048]{2,1,0:T(4,128)(2,1)S(1)} all-gather(bf16[1,4,2048]{2,1,0:T(4,128)(2,1)S(1)} %bitcast.88), channel_id=1, replica_groups=mesh['groups'=2,'tile'=4,'segment'=2,'mp'=2] {'tile'}, dimensions={0}, use_global_device_ids=true | all-gather | bytes 81920 | tf_op jit(solution)/shard_map/all_gather | solution.py:69
  42.8 2.8 convolution_convert_fusion
  46.4 8.4 %all_gather.27 = bf16[512,672]{0,1:T(8,128)(2,1)S(1)} all-gather(bf16[512,336]{0,1:T(8,128)(2,1)} %param.19), channel_id=1, replica_groups=mesh['groups'=2,'tile'=4,'segment'=2,'mp'=2] {'mp'}, dimensions={1}, use_global_device_ids=true | all-gather | bytes 1032192 | tf_op jit(solution)/shard_map/all_gather | solution.py:70
  56.1 4.2 %multiply_reduce_fusion.1 = (f32[64,16]{1,0:T(8,128)S(1)}, bf16[64,16,2048]{2,1,0:T(8,128)(2,1)}) fusion(f32[16,2048]{1,0:T(8,128)} %convert_element_type.165, bf16[64,16,48]{2,1,0:T(8,128)(2,1)S(1)} %dot_general.61, bf16[48,2048]{1,0:T(8,128)(2,1)} %param.15), kind=kOutput, calls=%fused_computation.7 | convolution fusion | flops 211811328 | bytes 4624384 | tf_op jit(solution)/shard_map/dot_general | solution.py:33
  60.4 29.6 %all-reduce.7.cloned.1.call-done = bf16[64,2048]{1,0:T(8,128)(2,1)} async-done(((bf16[64,2048]{1,0:T(8,128)(2,1)}), bf16[64,2048]{1,0:T(8,128)(2,1)}) %all-reduce.7.cloned.1.call-update) | async-done | bytes 262160 | tf_op jit(solution)/shard_map/psum | solution.py:75
  90.8 2.2 convolution_add_fusion
  93.0 5.3 %multiply_convert_fusion.1 = bf16[1024,2048]{1,0:T(8,128)(2,1)} fusion(f32[64,16,2048]{2,1,0:T(8,128)S(1)} %convolution_add_fusion, f32[1024]{0:T(1024)S(1)} %rsqrt.37), kind=kLoop, calls=%fused_computation.3 | loop fusion | flops 20971520 | bytes 12587008 | tf_op jit(solution)/shard_map/convert_element_type | solution.py:96
  98.3 7.2 %convolution_convert_fusion.1 = bf16[1024,672]{0,1:T(8,128)(2,1)} fusion(bf16[512,672]{0,1:T(8,128)(2,1)S(1)} %all_gather.27, bf16[1024,2048]{1,0:T(8,128)(2,1)} %multiply_convert_fusion.1, bf16[4096,512]{1,0:T(8,128)(2,1)} %param.18, s32[]{:T(128)S(6)} %select_n.37, bf16[1024,2048]{1,0:T(8,128)(2,1)} %bitcast.90, s32[]{:T(128)S(6)} %select_n.36, ...), kind=kOutput, calls=%fused_computation.22 | convolution fusion | flops 2854912000 | bytes 9404428 | tf_op jit(solution)/shard_map/dot_general | solution.py:33
  105.5 2.6 copy.40
  108.2 28.0 %reduce-scatter.3.cloned.1.call-done = bf16[1,4,64,672]{3,2,1,0:T(8,128)(2,1)} async-done(((bf16[4,4,64,672]{3,2,1,0:T(8,128)(2,1)}), bf16[1,4,64,672]{3,2,1,0:T(8,128)(2,1)}) %reduce-scatter.3.cloned.1.call-update) | async-done | bytes 344080 | tf_op jit(solution)/shard_map/reduce_scatter | solution.py:98
  138.7 1.9 reshape.268
  142.0 17.0 %reduce-scatter.5.cloned.1.call-done = bf16[1,64,672]{2,1,0:T(8,128)(2,1)} async-done(((bf16[4,64,672]{2,1,0:T(8,128)(2,1)}), bf16[1,64,672]{2,1,0:T(8,128)(2,1)}) %reduce-scatter.5.cloned.1.call-update) | async-done | bytes 86032 | tf_op jit(solution)/shard_map/reduce_scatter | solution.py:101
  160.0 15.8 %all_gather.28 = bf16[4,64,672]{2,1,0:T(8,128)(2,1)} all-gather(bf16[1,64,672]{2,1,0:T(8,128)(2,1)S(1)} %multiply_convert_fusion.6), channel_id=1, replica_groups=mesh['groups'=2,'tile'=4,'segment'=2,'mp'=2] {'tile'}, dimensions={0}, use_global_device_ids=true | all-gather | bytes 430080 | tf_op jit(solution)/shard_map/all_gather | solution.py:116
  176.2 17.2 %all-gather.6.cloned.1.call-done = bf16[16,64,672]{2,1,0:T(8,128)(2,1)} async-done(((bf16[4,64,672]{2,1,0:T(8,128)(2,1)}), bf16[16,64,672]{2,1,0:T(8,128)(2,1)}) %all-gather.6.cloned.1.call-update) | async-done | bytes 1376272 | tf_op jit(solution)/shard_map/all_gather | solution.py:116
  193.4 2.7 convolution_convert_fusion.2
  196.3 9.2 %multiply_reduce_fusion = (f32[1024]{0:T(1024)S(1)}, bf16[1024,2048]{1,0:T(8,128)(2,1)S(1)}) fusion(f32[64,16,2048]{2,1,0:T(8,128)} %copy-done.1, f32[1024]{0:T(1024)S(1)} %rsqrt.37, bf16[1024,512]{1,0:T(8,128)(2,1)S(1)} %convolution_convert_fusion.2, bf16[4096,512]{1,0:T(8,128)(2,1)S(1)} %copy-done.12, s32[]{:T(128)S(6)} %select_n.37), kind=kOutput, calls=%fused_computation.1 | convolution fusion | flops 2191522816 | bytes 15736836 | tf_op jit(solution)/shard_map/dot_general | solution.py:37
  207.5 2.0 fusion.21
  212.7 86.1 %all-reduce.9.cloned.1.call-done = bf16[64,768]{1,0:T(8,128)(2,1)} async-done(((bf16[64,768]{1,0:T(8,128)(2,1)}), bf16[64,768]{1,0:T(8,128)(2,1)}) %all-reduce.9.cloned.1.call-update) | async-done | bytes 98320 | tf_op jit(solution)/shard_map/psum | solution.py:126
  300.5 3.1 convolution_convert_fusion.3
  307.2 1.9 fusion.34
  310.2 17.2 %all-reduce.11.cloned.1.call-done = bf16[4,4,4,768]{3,2,0,1:T(4,128)(2,1)} async-done(((bf16[4,4,4,768]{3,2,0,1:T(4,128)(2,1)}), bf16[4,4,4,768]{3,2,0,1:T(4,128)(2,1)}) %all-reduce.11.cloned.1.call-update) | async-done | bytes 98320 | tf_op jit(solution)/shard_map/psum | solution.py:132
  329.7 13.3 %all-gather.3 = f32[4,224,16]{1,2,0:T(8,128)S(1)} all-gather(f32[1,224,16]{1,2,0:T(8,128)S(1)} %convolution_bitcast_fusion), channel_id=3, replica_groups=mesh['groups'=2,'tile'=4,'segment'=2,'mp'=2] {'tile'}, dimensions={0}, use_global_device_ids=true | all-gather | bytes 71680 | tf_op jit(solution)/shard_map/all_gather | solution.py:140
  (102 shorter events, 26.9 us)
Async XLA Ops:
  7.2 21.0 %copy-start = (bf16[1536,768]{1,0:T(8,128)(2,1)S(1)}, bf16[1536,768]{1,0:T(8,128)(2,1)}, u32[]{:S(2)}) copy-start(bf16[1536,768]{1,0:T(8,128)(2,1)} %param.14) | copy-start | bytes 7077892
  7.2 22.3 %copy-start.10 = (bf16[4,2048]{1,0:T(4,128)(2,1)S(1)}, bf16[4,2048]{1,0:T(4,128)(2,1)}, u32[]{:S(2)}) copy-start(bf16[4,2048]{1,0:T(4,128)(2,1)} %param.16) | copy-start | bytes 49156
  7.2 47.6 %all-reduce.5.cloned.1.call-start = ((), (), s32[]{:S(2)}) async-start(), calls=%async_computation.2 | async-start | bytes 196608 | tf_op jit(solution)/shard_map/psum | solution.py:81
  7.2 35.6 %copy-start.8 = (bf16[48,2048]{1,0:T(8,128)(2,1)S(1)}, bf16[48,2048]{1,0:T(8,128)(2,1)}, u32[]{:S(2)}) copy-start(bf16[48,2048]{1,0:T(8,128)(2,1)} %param.15) | copy-start | bytes 589828
  25.2 4.3 %copy-start.7 = (bf16[64,768]{1,0:T(8,128)(2,1)}, bf16[64,768]{1,0:T(8,128)(2,1)S(1)}, u32[]{:S(2)}) copy-start(bf16[64,768]{1,0:T(8,128)(2,1)S(1)} %multiply_convert_fusion.7) | copy-start | bytes 294916
  27.4 0.8 copy-start.3
  29.4 60.6 %all-reduce.7.cloned.1.call-start = ((), (), s32[]{:S(2)}) async-start(), calls=%async_computation.3 | async-start | bytes 524288 | tf_op jit(solution)/shard_map/psum | solution.py:75
  45.6 90.6 %reduce-scatter.3.cloned.1.call-start = ((), (), s32[]{:S(2)}) async-start(), calls=%async_computation.4 | async-start | bytes 1966080 | tf_op jit(solution)/shard_map/reduce_scatter | solution.py:98
  54.7 43.5 %copy-start.6 = (bf16[512,672]{0,1:T(8,128)(2,1)}, bf16[512,672]{0,1:T(8,128)(2,1)S(1)}, u32[]{:S(2)}) copy-start(bf16[512,672]{0,1:T(8,128)(2,1)S(1)} %all_gather.27) | copy-start | bytes 2064388
  93.0 5.3 %copy-start.1 = (f32[64,16,2048]{2,1,0:T(8,128)}, f32[64,16,2048]{2,1,0:T(8,128)S(1)}, u32[]{:S(2)}) copy-start(f32[64,16,2048]{2,1,0:T(8,128)S(1)} %convolution_add_fusion) | copy-start | bytes 25165828
  105.5 30.8 %copy-start.11 = (s32[2,32]{1,0:T(2,128)S(1)}, s32[2,32]{1,0:T(2,128)}, u32[]{:S(2)}) copy-start(s32[2,32]{1,0:T(2,128)} %param.11) | copy-start | bytes 772
  105.5 31.2 %copy-start.2 = (bf16[2,8,48,224]{3,2,1,0:T(8,128)(2,1)S(1)}, bf16[2,8,48,224]{3,2,1,0:T(8,128)(2,1)}, u32[]{:S(2)}) copy-start(bf16[2,8,48,224]{3,2,1,0:T(8,128)(2,1)} %param.10) | copy-start | bytes 1032196
  108.1 50.8 %reduce-scatter.5.cloned.1.call-start = ((), (), s32[]{:S(2)}) async-start(), calls=%async_computation.5 | async-start | bytes 491520 | tf_op jit(solution)/shard_map/reduce_scatter | solution.py:101
  136.2 57.2 %all-gather.6.cloned.1.call-start = ((), (), s32[]{:S(2)}) async-start(), calls=%async_computation.8 | async-start | bytes 1966080 | tf_op jit(solution)/shard_map/all_gather | solution.py:116
  175.8 123.0 %all-reduce.9.cloned.1.call-start = ((), (), s32[]{:S(2)}) async-start(), calls=%async_computation.6 | async-start | bytes 196608 | tf_op jit(solution)/shard_map/psum | solution.py:126
  193.4 2.9 copy-start.12
  196.3 9.2 %copy-start.9 = (bf16[48,2048]{1,0:T(8,128)(2,1)S(1)}, bf16[48,2048]{1,0:T(8,128)(2,1)}, u32[]{:S(2)}) copy-start(bf16[48,2048]{1,0:T(8,128)(2,1)} %param.15) | copy-start | bytes 589828
  196.3 9.7 %copy-start.13 = (bf16[64,16,2048]{2,1,0:T(8,128)(2,1)S(1)}, bf16[64,16,2048]{2,1,0:T(8,128)(2,1)}, u32[]{:S(2)}) copy-start(bf16[64,16,2048]{2,1,0:T(8,128)(2,1)} %get-tuple-element.6) | copy-start | bytes 12582916
  206.0 1.5 copy-start.5
  207.5 91.4 %copy-start.4 = (f32[64,1536]{1,0:T(8,128)S(1)}, f32[64,1536]{1,0:T(8,128)}, u32[]{:S(2)}) copy-start(f32[64,1536]{1,0:T(8,128)} %copy-done.3) | copy-start | bytes 1179652
  211.5 115.9 %all-reduce.11.cloned.1.call-start = ((), (), s32[]{:S(2)}) async-start(), calls=%async_computation.7 | async-start | bytes 196608 | tf_op jit(solution)/shard_map/psum | solution.py:132
Sparse Core Ops, SparseCore 0:
  29.5 22.1 all-reduce.4
  54.6 35.3 all-reduce.6
  108.3 27.9 reduce-scatter.2
  138.3 20.5 reduce-scatter.4
  175.9 17.4 all-gather.5
  211.6 87.1 all-reduce.8
  307.3 20.0 all-reduce.10
where the time goes:
time: 351 us; the launch traced here: 350 us
  waiting for transfers between devices  195 us (56%)
  blocking collectives  65.8 us (19%)
  matrix products  45.8 us (13%)
  local copies, waits for them, and re-layouts  15.7 us (4%)
  between operations  15.2 us (4%)
  other arithmetic  12.3 us (4%)
    psum x1, waiting for transfers between devices, body(): lax.psum(grad_tok.reshape(rows, student).astype(BF), ('tile', 'segment',...  86.1 us
    psum x1, waiting for transfers between devices, body(): folded = lax.psum(dot(embed_z, d_in).astype(BF), 'tile')  29.6 us
    reduce_scatter x1, waiting for transfers between devices, body(): lax.psum_scatter(partial.reshape(S * M, T, share * codes, -1), ('segment'...  28 us
    dot_general x7, matrix products, dot(): return jnp.dot(a, b, preferred_element_type=F32)  21.1 us
    dot_general x7, matrix products, dot_t(): lax.dot_general(a, b, (((1,), (1,)), ((), ())), preferred_element_type=F32)  20.7 us
    all_gather x1, waiting for transfers between devices, body(): lax.all_gather(lax.all_gather(grad_own, 'tile'), ('segment', 'mp'))  17.2 us
    psum x1, waiting for transfers between devices, body(): grad_normed = lax.psum(dot_t(grad_act, enc_in).astype(BF), 'mp').astype(F32)  17.2 us
    reduce_scatter x1, waiting for transfers between devices, body(): own = lax.psum_scatter(own, 'tile', scatter_dimension=0).astype(F32)  17 us
  transfers between devices with their start and end apart: 7, of which 6 were waited for; matrix products, arithmetic and copies ran while one was open for 5% of the time, Pallas kernels for 0%

commit v1 on v0

--- a/solution.py
+++ b/solution.py
@@ -5,6 +5,18 @@
 
 BF = jnp.bfloat16
 F32 = jnp.float32
+
+
+def gather_by_bits(value, axis, dim):
+    ways, here, step = (lax.axis_size(axis), lax.axis_index(axis), value.shape[dim])
+    line, have = (value, 1)
+    while have < ways:
+        line = jnp.concatenate(
+            [line, lax.ppermute(line, axis, [(d, (d - have) % ways) for d in range(ways)])],
+            axis=dim,
+        )
+        have = 2 * have
+    return jnp.roll(line, here * step, axis=dim)
 
 
 def inv_rms(values):
@@ -67,7 +79,7 @@
     feats = lax.all_gather(feat_local, "tile")
     feats = feats.reshape(T, S, M, share, student).transpose(1, 2, 0, 3, 4).reshape(rows, student)
     band_all = lax.all_gather(band_embed, "tile", tiled=True)
-    head_full = lax.all_gather(head, "mp", axis=1, tiled=True)
+    head_full = gather_by_bits(head, "mp", 1)
     embed = jnp.concatenate([tok_embed, band_all], axis=0)
     embed_z = lax.dynamic_slice_in_dim(embed, tile * dt, dt, 1)
     d_in = lax.dynamic_slice_in_dim(dec_in, seg * hid, hid, 1)

time: 351 us -> 355 us (1.011)
  blocking collectives: 65.8 us -> 57.3 us
  waiting for transfers between devices: 195 us -> 202 us
    all_gather x1 -> x0, blocking collectives: 8.39 us -> none  [body(): head_full = lax.all_gather(head, 'mp', axis=1, tiled=True)]
    psum x1, waiting for transfers between devices: 0.01 us -> 3.98 us  [body(): summed = lax.psum(dot(act_out, enc_out).astype(BF), 'mp').astype(F32)]
  transfers between devices with their start and end apart: 7 -> 8, of which waited for: 6 -> 7; matrix products, arithmetic and copies ran while one was open for 5% -> 7% of each run, Pallas kernels for 0% -> 0%
where the time goes in v1:
time: 355 us; the launch traced here: 354 us
  waiting for transfers between devices  202 us (57%)
  blocking collectives  57.3 us (16%)
  matrix products  45.7 us (13%)
  local copies, waits for them, and re-layouts  16.6 us (5%)
  between operations  15.2 us (4%)
  other arithmetic  14.8 us (4%)
    psum x1, waiting for transfers between devices, body(): lax.psum(grad_tok.reshape(rows, student).astype(BF), ('tile', 'segment',...  86.1 us
    psum x1, waiting for transfers between devices, body(): folded = lax.psum(dot(embed_z, d_in).astype(BF), 'tile')  32.9 us
    reduce_scatter x1, waiting for transfers between devices, body(): lax.psum_scatter(partial.reshape(S * M, T, share * codes, -1), ('segment'...  28.1 us
    dot_general x7, matrix products, dot(): return jnp.dot(a, b, preferred_element_type=F32)  21 us
    dot_general x7, matrix products, dot_t(): lax.dot_general(a, b, (((1,), (1,)), ((), ())), preferred_element_type=F32)  20.7 us
    all_gather x1, waiting for transfers between devices, body(): lax.all_gather(lax.all_gather(grad_own, 'tile'), ('segment', 'mp'))  17.4 us
    psum x1, waiting for transfers between devices, body(): grad_normed = lax.psum(dot_t(grad_act, enc_in).astype(BF), 'mp').astype(F32)  17.2 us
    reduce_scatter x1, waiting for transfers between devices, body(): own = lax.psum_scatter(own, 'tile', scatter_dimension=0).astype(F32)  16.8 us
  transfers between devices with their start and end apart: 8, of which 7 were waited for; matrix products, arithmetic and copies ran while one was open for 7% of the time, Pallas kernels for 0%

profile of v1, /device:TPU:0, one launch (start us, length us, event | category | flops | bytes accessed | tf_op | source)
XLA Modules:
  0.0 353.9 jit_solution(9914980210259476359)
XLA Ops:
  9.6 15.0 %all_gather.22 = bf16[4,16,768]{2,1,0:T(8,128)(2,1)S(1)} all-gather(bf16[1,16,768]{2,1,0:T(8,128)(2,1)S(1)} %all_gather_reshape.3), channel_id=1, replica_groups=mesh['groups'=2,'tile'=4,'segment'=2,'mp'=2] {'tile'}, dimensions={0}, use_global_device_ids=true | all-gather | bytes 122880 | tf_op jit(solution)/shard_map/all_gather | solution.py:79
  25.2 2.2 fusion.53
  31.0 13.1 %all-gather.2 = bf16[4,4,2048]{2,1,0:T(4,128)(2,1)S(1)} all-gather(bf16[1,4,2048]{2,1,0:T(4,128)(2,1)S(1)} %bitcast.88), channel_id=1, replica_groups=mesh['groups'=2,'tile'=4,'segment'=2,'mp'=2] {'tile'}, dimensions={0}, use_global_device_ids=true | all-gather | bytes 81920 | tf_op jit(solution)/shard_map/all_gather | solution.py:81
  44.2 2.8 convolution_convert_fusion
  47.7 4.0 %all-reduce.5.cloned.1.call-done = bf16[64,768]{1,0:T(8,128)(2,1)} async-done(((bf16[64,768]{1,0:T(8,128)(2,1)}), bf16[64,768]{1,0:T(8,128)(2,1)}) %all-reduce.5.cloned.1.call-update) | async-done | bytes 98320 | tf_op jit(solution)/shard_map/psum | solution.py:93
  52.9 4.1 %multiply_reduce_fusion.1 = (f32[64,16]{1,0:T(8,128)S(1)}, bf16[64,16,2048]{2,1,0:T(8,128)(2,1)}) fusion(f32[16,2048]{1,0:T(8,128)} %convert_element_type.165, bf16[64,16,48]{2,1,0:T(8,128)(2,1)S(1)} %dot_general.61, bf16[48,2048]{1,0:T(8,128)(2,1)S(1)} %copy-done.9), kind=kOutput, calls=%fused_computation.7 | convolution fusion | flops 211811328 | bytes 4624384 | tf_op jit(solution)/shard_map/dot_general | solution.py:45
  57.1 32.9 %all-reduce.7.cloned.1.call-done = bf16[64,2048]{1,0:T(8,128)(2,1)} async-done(((bf16[64,2048]{1,0:T(8,128)(2,1)}), bf16[64,2048]{1,0:T(8,128)(2,1)}) %all-reduce.7.cloned.1.call-update) | async-done | bytes 262160 | tf_op jit(solution)/shard_map/psum | solution.py:87
  90.8 2.2 convolution_add_fusion
  93.0 5.3 %multiply_convert_fusion.1 = bf16[1024,2048]{1,0:T(8,128)(2,1)} fusion(f32[64,16,2048]{2,1,0:T(8,128)S(1)} %convolution_add_fusion, f32[1024]{0:T(1024)S(1)} %rsqrt.37), kind=kLoop, calls=%fused_computation.3 | loop fusion | flops 20971520 | bytes 12587008 | tf_op jit(solution)/shard_map/convert_element_type | solution.py:108
  98.3 2.6 fusion.28
  101.8 7.2 %convolution_convert_fusion.1 = bf16[1024,672]{0,1:T(8,128)(2,1)} fusion(bf16[512,672]{0,1:T(8,128)(2,1)S(1)} %fusion.28, bf16[1024,2048]{1,0:T(8,128)(2,1)} %multiply_convert_fusion.1, bf16[4096,512]{1,0:T(8,128)(2,1)} %param.18, s32[]{:T(128)S(6)} %select_n.50, bf16[1024,2048]{1,0:T(8,128)(2,1)} %bitcast.90, s32[]{:T(128)S(6)} %select_n.49, ...), kind=kOutput, calls=%fused_computation.22 | convolution fusion | flops 2854912000 | bytes 9404428 | tf_op jit(solution)/shard_map/dot_general | solution.py:45
  109.0 2.6 copy.40
  111.7 28.1 %reduce-scatter.3.cloned.1.call-done = bf16[1,4,64,672]{3,2,1,0:T(8,128)(2,1)} async-done(((bf16[4,4,64,672]{3,2,1,0:T(8,128)(2,1)}), bf16[1,4,64,672]{3,2,1,0:T(8,128)(2,1)}) %reduce-scatter.3.cloned.1.call-update) | async-done | bytes 344080 | tf_op jit(solution)/shard_map/reduce_scatter | solution.py:110
  142.4 1.9 reshape.268
  145.7 16.8 %reduce-scatter.5.cloned.1.call-done = bf16[1,64,672]{2,1,0:T(8,128)(2,1)} async-done(((bf16[4,64,672]{2,1,0:T(8,128)(2,1)}), bf16[1,64,672]{2,1,0:T(8,128)(2,1)}) %reduce-scatter.5.cloned.1.call-update) | async-done | bytes 86032 | tf_op jit(solution)/shard_map/reduce_scatter | solution.py:113
  163.5 15.8 %all_gather.24 = bf16[4,64,672]{2,1,0:T(8,128)(2,1)} all-gather(bf16[1,64,672]{2,1,0:T(8,128)(2,1)S(1)} %multiply_convert_fusion.6), channel_id=1, replica_groups=mesh['groups'=2,'tile'=4,'segment'=2,'mp'=2] {'tile'}, dimensions={0}, use_global_device_ids=true | all-gather | bytes 430080 | tf_op jit(solution)/shard_map/all_gather | solution.py:128
  179.6 17.4 %all-gather.6.cloned.1.call-done = bf16[16,64,672]{2,1,0:T(8,128)(2,1)} async-done(((bf16[4,64,672]{2,1,0:T(8,128)(2,1)}), bf16[16,64,672]{2,1,0:T(8,128)(2,1)}) %all-gather.6.cloned.1.call-update) | async-done | bytes 1376272 | tf_op jit(solution)/shard_map/all_gather | solution.py:128
  197.0 2.7 convolution_convert_fusion.2
  199.8 9.2 %multiply_reduce_fusion = (f32[1024]{0:T(1024)S(1)}, bf16[1024,2048]{1,0:T(8,128)(2,1)S(1)}) fusion(f32[64,16,2048]{2,1,0:T(8,128)} %copy-done.1, f32[1024]{0:T(1024)S(1)} %rsqrt.37, bf16[1024,512]{1,0:T(8,128)(2,1)S(1)} %convolution_convert_fusion.2, bf16[4096,512]{1,0:T(8,128)(2,1)S(1)} %copy-done.13, s32[]{:T(128)S(6)} %select_n.50), kind=kOutput, calls=%fused_computation.1 | convolution fusion | flops 2191522816 | bytes 15736836 | tf_op jit(solution)/shard_map/dot_general | solution.py:49
  211.0 2.0 fusion.21
  216.2 86.1 %all-reduce.9.cloned.1.call-done = bf16[64,768]{1,0:T(8,128)(2,1)} async-done(((bf16[64,768]{1,0:T(8,128)(2,1)}), bf16[64,768]{1,0:T(8,128)(2,1)}) %all-reduce.9.cloned.1.call-update) | async-done | bytes 98320 | tf_op jit(solution)/shard_map/psum | solution.py:138
  304.0 3.1 convolution_convert_fusion.3
  313.6 17.2 %all-reduce.11.cloned.1.call-done = bf16[4,4,4,768]{3,2,0,1:T(4,128)(2,1)} async-done(((bf16[4,4,4,768]{3,2,0,1:T(4,128)(2,1)}), bf16[4,4,4,768]{3,2,0,1:T(4,128)(2,1)}) %all-reduce.11.cloned.1.call-update) | async-done | bytes 98320 | tf_op jit(solution)/shard_map/psum | solution.py:144
  333.1 13.3 %all-gather.3 = f32[4,224,16]{1,2,0:T(8,128)S(1)} all-gather(f32[1,224,16]{1,2,0:T(8,128)S(1)} %convolution_bitcast_fusion), channel_id=3, replica_groups=mesh['groups'=2,'tile'=4,'segment'=2,'mp'=2] {'tile'}, dimensions={0}, use_global_device_ids=true | all-gather | bytes 71680 | tf_op jit(solution)/shard_map/all_gather | solution.py:152
  (106 shorter events, 31.2 us)
Async XLA Ops:
  7.2 21.0 %copy-start = (bf16[1536,768]{1,0:T(8,128)(2,1)S(1)}, bf16[1536,768]{1,0:T(8,128)(2,1)}, u32[]{:S(2)}) copy-start(bf16[1536,768]{1,0:T(8,128)(2,1)} %param.14) | copy-start | bytes 7077892
  7.2 22.3 %copy-start.8 = (bf16[512,336]{0,1:T(8,128)(2,1)S(1)}, bf16[512,336]{0,1:T(8,128)(2,1)}, u32[]{:S(2)}) copy-start(bf16[512,336]{0,1:T(8,128)(2,1)} %param.19) | copy-start | bytes 1032196
  7.2 23.8 %copy-start.11 = (bf16[4,2048]{1,0:T(4,128)(2,1)S(1)}, bf16[4,2048]{1,0:T(4,128)(2,1)}, u32[]{:S(2)}) copy-start(bf16[4,2048]{1,0:T(4,128)(2,1)} %param.16) | copy-start | bytes 49156
  7.2 44.5 %all-reduce.5.cloned.1.call-start = ((), (), s32[]{:S(2)}) async-start(), calls=%async_computation.2 | async-start | bytes 196608 | tf_op jit(solution)/shard_map/psum | solution.py:93
  7.2 36.9 %copy-start.9 = (bf16[48,2048]{1,0:T(8,128)(2,1)S(1)}, bf16[48,2048]{1,0:T(8,128)(2,1)}, u32[]{:S(2)}) copy-start(bf16[48,2048]{1,0:T(8,128)(2,1)} %param.15) | copy-start | bytes 589828
  25.2 5.8 %copy-start.7 = (bf16[64,768]{1,0:T(8,128)(2,1)}, bf16[64,768]{1,0:T(8,128)(2,1)S(1)}, u32[]{:S(2)}) copy-start(bf16[64,768]{1,0:T(8,128)(2,1)S(1)} %multiply_convert_fusion.7) | copy-start | bytes 294916
  27.4 0.8 copy-start.3
  29.4 60.6 %all-reduce.7.cloned.1.call-start = ((), (), s32[]{:S(2)}) async-start(), calls=%async_computation.3 | async-start | bytes 524288 | tf_op jit(solution)/shard_map/psum | solution.py:87
  29.5 68.8 %collective-permute-start = (bf16[512,336]{0,1:T(8,128)(2,1)S(1)}, bf16[512,336]{0,1:T(8,128)(2,1)}, u32[]{:S(2)}, u32[]{:S(2)}) collective-permute-start(bf16[512,336]{0,1:T(8,128)(2,1)S(1)} %copy-done.8), channel_id=1, source_target_pairs={{0,1},{1,0},{2,3},{3,2},{4,5},{5,4},{6,7},{7,6},{8,9},{9,8},{10,11... | collective-permute-start | bytes 1032200 | tf_op jit(solution)/shard_map/ppermute | solution.py:15
  47.0 92.7 %reduce-scatter.3.cloned.1.call-start = ((), (), s32[]{:S(2)}) async-start(), calls=%async_computation.4 | async-start | bytes 1966080 | tf_op jit(solution)/shard_map/reduce_scatter | solution.py:110
  93.0 5.3 %copy-start.1 = (f32[64,16,2048]{2,1,0:T(8,128)}, f32[64,16,2048]{2,1,0:T(8,128)S(1)}, u32[]{:S(2)}) copy-start(f32[64,16,2048]{2,1,0:T(8,128)S(1)} %convolution_add_fusion) | copy-start | bytes 25165828
  100.9 0.9 copy-start.6
  109.0 31.0 %copy-start.12 = (s32[2,32]{1,0:T(2,128)S(1)}, s32[2,32]{1,0:T(2,128)}, u32[]{:S(2)}) copy-start(s32[2,32]{1,0:T(2,128)} %param.11) | copy-start | bytes 772
  109.0 31.4 %copy-start.2 = (bf16[2,8,48,224]{3,2,1,0:T(8,128)(2,1)S(1)}, bf16[2,8,48,224]{3,2,1,0:T(8,128)(2,1)}, u32[]{:S(2)}) copy-start(bf16[2,8,48,224]{3,2,1,0:T(8,128)(2,1)} %param.10) | copy-start | bytes 1032196
  111.6 50.9 %reduce-scatter.5.cloned.1.call-start = ((), (), s32[]{:S(2)}) async-start(), calls=%async_computation.5 | async-start | bytes 491520 | tf_op jit(solution)/shard_map/reduce_scatter | solution.py:113
  139.8 57.2 %all-gather.6.cloned.1.call-start = ((), (), s32[]{:S(2)}) async-start(), calls=%async_computation.8 | async-start | bytes 1966080 | tf_op jit(solution)/shard_map/all_gather | solution.py:128
  179.3 122.9 %all-reduce.9.cloned.1.call-start = ((), (), s32[]{:S(2)}) async-start(), calls=%async_computation.6 | async-start | bytes 196608 | tf_op jit(solution)/shard_map/psum | solution.py:138
  197.0 2.9 copy-start.13
  199.8 9.2 %copy-start.10 = (bf16[48,2048]{1,0:T(8,128)(2,1)S(1)}, bf16[48,2048]{1,0:T(8,128)(2,1)}, u32[]{:S(2)}) copy-start(bf16[48,2048]{1,0:T(8,128)(2,1)} %param.15) | copy-start | bytes 589828
  199.8 9.7 %copy-start.14 = (bf16[64,16,2048]{2,1,0:T(8,128)(2,1)S(1)}, bf16[64,16,2048]{2,1,0:T(8,128)(2,1)}, u32[]{:S(2)}) copy-start(bf16[64,16,2048]{2,1,0:T(8,128)(2,1)} %get-tuple-element.6) | copy-start | bytes 12582916
  209.5 1.5 copy-start.5
  211.0 91.3 %copy-start.4 = (f32[64,1536]{1,0:T(8,128)S(1)}, f32[64,1536]{1,0:T(8,128)}, u32[]{:S(2)}) copy-start(f32[64,1536]{1,0:T(8,128)} %copy-done.3) | copy-start | bytes 1179652
  215.0 115.8 %all-reduce.11.cloned.1.call-start = ((), (), s32[]{:S(2)}) async-start(), calls=%async_computation.7 | async-start | bytes 196608 | tf_op jit(solution)/shard_map/psum | solution.py:144
Sparse Core Ops, SparseCore 0:
  29.5 22.1 all-reduce.4
  54.6 35.3 all-reduce.6
  111.8 27.9 reduce-scatter.2
  141.9 20.5 reduce-scatter.4
  179.5 17.4 all-gather.5
  215.1 87.0 all-reduce.8
  310.8 20.0 all-reduce.10
